TPU v7x, 32 devices: a whole 2x2x4 slice. The times are simulated.
32 devices in a mesh: member: 8 (over y, x, core), space: 4 (over z).
Axes of the slice: x: 2, y: 2, z: 4, core: 2. Of those that a mesh axis runs over, the one named last changes fastest.
Arguments:
- realization_channels: bfloat16 [8, 4096, 1024], P('member', 'space'), may hold values from -6 to 6
- node_gain: bfloat16 [1024], replicated, may hold values from 0.5 to 1.5
- w_self: bfloat16 [1024, 1024], replicated, may hold values from -0.1875 to 0.1875
- w_neighbour: bfloat16 [1024, 1024], replicated, may hold values from -0.1875 to 0.1875
- w_out: bfloat16 [1024, 1024], replicated, may hold values from -0.1875 to 0.1875
- readout_map: bfloat16 [100, 1024], replicated, may hold values from -0.1875 to 0.1875
- edge_index: int32 [4096, 8], P('space'), may hold values from 0 to 1279, as said below
- verifying_truth: float32 [100, 4096], P(None, 'space'), may hold values from -6 to 6
- var_weight: float32 [100], replicated, may hold values from 0.3 to 3
- area_weight: float32 [4096], P('space'), may hold values from 0.3 to 3
Outputs:
- grad_hidden: bfloat16 [8, 4096, 1024], P('member', 'space')
- grad_decoder: float32 [100, 1024], replicated
Inputs may be any that keep to these rules, and one draw needn't show every extreme that they name: `edge_index`: entry e of a node at position i of its shard's 1024 nodes lies within 128 of i + 128.
All inputs are finite; a program needn't handle non-finite values.
Results may differ from a plain program's by a relative error of at most 0.012.
The roundings to bfloat16 on the way count: a program that leaves them out, or rounds other values in their place, can miss the bound.
Values may be sent and summed in bfloat16 or wider, within the bound.
A program may use at most 128 MiB of HBM per device.

v0:
```python
import jax
import jax.numpy as jnp
from jax import lax
from jax.sharding import PartitionSpec as P

K = 8
HALO = 128


TAU = 0.05
ALPHA = 0.95


def padded(block, sides, width):
    for axis, dim in sides:
        count = lax.axis_size(axis)
        forward = [(i, i + 1) for i in range(count - 1)]
        backward = [(target, source) for source, target in forward]
        low = lax.ppermute(
            lax.slice_in_dim(block, block.shape[dim] - width, None, axis=dim), axis, forward
        )
        high = lax.ppermute(lax.slice_in_dim(block, 0, width, axis=dim), axis, backward)
        block = jnp.concatenate([low, block, high], axis=dim)
    return block


def softened_sign(diff):
    return diff / jnp.sqrt(diff * diff + TAU * TAU)


def local(
    realization_channels,
    node_gain,
    w_self,
    w_neighbour,
    w_out,
    readout_map,
    edge_index,
    verifying_truth,
    var_weight,
    area_weight,
):
    values = realization_channels[0].astype(jnp.float32)
    node_count = values.shape[0]
    scale = lax.rsqrt(jnp.mean(values * values, axis=-1, keepdims=True) + 1e-06)
    normed = (values * scale * node_gain.astype(jnp.float32)).astype(jnp.bfloat16)
    extended = padded(normed, (("space", 0),), HALO)
    summed = jnp.zeros(values.shape, jnp.float32)
    for column in range(K):
        summed = summed + extended[edge_index[:, column]].astype(jnp.float32)
    neighbour_mean = (summed / K).astype(jnp.bfloat16)
    inside = jnp.dot(normed, w_self, preferred_element_type=jnp.float32) + jnp.dot(
        neighbour_mean, w_neighbour, preferred_element_type=jnp.float32
    )
    activated = jax.nn.gelu(inside).astype(jnp.bfloat16)
    latent_channels = (
        values + jnp.dot(activated, w_out, preferred_element_type=jnp.float32)
    ).astype(jnp.bfloat16)
    prediction_field = lax.dot_general(
        readout_map, latent_channels, (((1,), (1,)), ((), ())), preferred_element_type=jnp.float32
    )
    members = lax.axis_size("member")
    eps = (1.0 - ALPHA) / members
    couple_factor = (1.0 - eps) / (members - 1)
    linear_operator = var_weight[:, None] * area_weight[None, :]
    entire_collection = lax.all_gather(prediction_field[None], "member", axis=0, tiled=True)
    collective_dispersion = jnp.sum(
        softened_sign(prediction_field[None] - entire_collection), axis=0
    )
    couple_derivatives = (
        linear_operator
        * (
            softened_sign(prediction_field - verifying_truth)
            - couple_factor * collective_dispersion
        )
    ).astype(jnp.bfloat16)
    grad_hidden = lax.dot_general(
        couple_derivatives,
        readout_map,
        (((0,), (0,)), ((), ())),
        preferred_element_type=jnp.float32,
    ).astype(jnp.bfloat16)
    local_decoder = jnp.dot(couple_derivatives, latent_channels, preferred_element_type=jnp.float32)
    total_decoder = lax.psum(local_decoder, ("member", "space"))
    all_nodes = node_count * lax.axis_size("space")
    grad_decoder = total_decoder / jnp.sqrt(jnp.float32(members * all_nodes))
    return (grad_hidden[None], grad_decoder)


def solution(mesh):
    return jax.shard_map(
        local,
        mesh=mesh,
        in_specs=(
            P("member", "space", None),
            P(),
            P(),
            P(),
            P(),
            P(),
            P("space", None),
            P(None, "space"),
            P(),
            P("space"),
        ),
        out_specs=(P("member", "space", None), P()),
        check_vma=False,
    )
```

profile of v0, /device:TPU:0, one launch (start us, length us, event | category | flops | bytes accessed | tf_op | source)
XLA Modules:
  0.0 284.3 jit_solution(14216311280576832688)
XLA Ops:
  7.2 0.0 copy-start
  7.2 0.0 all-gather.4.cloned.1.call-start
  7.2 0.0 copy-start.1
  7.2 0.8 convert_element_type.53
  8.1 2.2 fusion.8
  10.3 0.0 copy-start.6
  10.3 0.5 fusion.10
  10.9 4.9 %collective-permute-start = (bf16[128,1024]{1,0:T(8,128)(2,1)S(1)}, bf16[128,1024]{1,0:T(8,128)(2,1)S(1)}, u32[]{:S(2)}, u32[]{:S(2)}) collective-permute-start(bf16[128,1024]{1,0:T(8,128)(2,1)S(1)} %get-tuple-element.2), channel_id=1, source_target_pairs={{0,1},{1,2},{2,3},{4,5},{5,6},{6,7},{8,9},{9,10},{10,11},{12,13},{... | collective-permute-start | bytes 786440 | tf_op jit(solution)/shard_map/ppermute | solution.py:19
  15.8 1.3 collective-permute-start.1
  17.3 4.3 %fusion.29 = f32[1024,1024]{1,0:T(8,128)} fusion(bf16[1024,1024]{1,0:T(8,128)(2,1)S(1)} %fusion.10, bf16[1024,1024]{1,0:T(8,128)(2,1)S(1)} %copy-done), kind=kOutput, calls=%fused_computation.60 | convolution fusion | flops 2147483648 | bytes 8388608 | tf_op jit(solution)/shard_map/dot_general | solution.py:52
  21.6 3.9 %collective-permute-done.1 = bf16[128,1024]{1,0:T(8,128)(2,1)S(1)} collective-permute-done((bf16[128,1024]{1,0:T(8,128)(2,1)S(1)}, bf16[128,1024]{1,0:T(8,128)(2,1)S(1)}, u32[]{:S(2)}, u32[]{:S(2)}) %collective-permute-start.1) | collective-permute-done | bytes 262176 | tf_op jit(solution)/shard_map/ppermute | solution.py:22
  25.5 1.8 pad_maximum_fusion
  27.3 8.3 %gather_fusion.7 = bf16[1024,1024]{1,0:T(8,128)(2,1)} fusion(bf16[1280,1024]{1,0:T(8,128)(2,1)} %pad_maximum_fusion, s32[1024]{0:T(1024)S(1)} %broadcast_clamp_fusion), kind=kCustom, calls=%fused_computation.7 | custom fusion | bytes 4198400 | tf_op jit(solution)/shard_map/gather | solution.py:50
  35.5 8.1 %gather_fusion.6 = bf16[1024,1024]{1,0:T(8,128)(2,1)} fusion(bf16[1280,1024]{1,0:T(8,128)(2,1)} %pad_maximum_fusion, s32[1024]{0:T(1024)S(1)} %broadcast_clamp_fusion.1), kind=kCustom, calls=%fused_computation.6 | custom fusion | bytes 4198400 | tf_op jit(solution)/shard_map/gather | solution.py:50
  43.7 8.1 %gather_fusion.5 = bf16[1024,1024]{1,0:T(8,128)(2,1)} fusion(bf16[1280,1024]{1,0:T(8,128)(2,1)} %pad_maximum_fusion, s32[1024]{0:T(1024)S(1)} %broadcast_clamp_fusion.2), kind=kCustom, calls=%fused_computation.5 | custom fusion | bytes 4198400 | tf_op jit(solution)/shard_map/gather | solution.py:50
  51.8 8.1 %gather_fusion.4 = bf16[1024,1024]{1,0:T(8,128)(2,1)} fusion(bf16[1280,1024]{1,0:T(8,128)(2,1)} %pad_maximum_fusion, s32[1024]{0:T(1024)S(1)} %broadcast_clamp_fusion.3), kind=kCustom, calls=%fused_computation.4 | custom fusion | bytes 4198400 | tf_op jit(solution)/shard_map/gather | solution.py:50
  59.9 8.1 %gather_fusion.3 = bf16[1024,1024]{1,0:T(8,128)(2,1)} fusion(bf16[1280,1024]{1,0:T(8,128)(2,1)} %pad_maximum_fusion, s32[1024]{0:T(1024)S(1)} %broadcast_clamp_fusion.4), kind=kCustom, calls=%fused_computation.3 | custom fusion | bytes 4198400 | tf_op jit(solution)/shard_map/gather | solution.py:50
  68.0 8.1 %gather_fusion.2 = bf16[1024,1024]{1,0:T(8,128)(2,1)} fusion(bf16[1280,1024]{1,0:T(8,128)(2,1)} %pad_maximum_fusion, s32[1024]{0:T(1024)S(1)} %broadcast_clamp_fusion.5), kind=kCustom, calls=%fused_computation.2 | custom fusion | bytes 4198400 | tf_op jit(solution)/shard_map/gather | solution.py:50
  76.2 8.1 %gather_fusion.1 = bf16[1024,1024]{1,0:T(8,128)(2,1)} fusion(bf16[1280,1024]{1,0:T(8,128)(2,1)} %pad_maximum_fusion, s32[1024]{0:T(1024)S(1)} %broadcast_clamp_fusion.6), kind=kCustom, calls=%fused_computation.1 | custom fusion | bytes 4198400 | tf_op jit(solution)/shard_map/gather | solution.py:50
  84.3 8.1 %gather_fusion = bf16[1024,1024]{1,0:T(8,128)(2,1)} fusion(bf16[1280,1024]{1,0:T(8,128)(2,1)} %pad_maximum_fusion, s32[1024]{0:T(1024)S(1)} %broadcast_clamp_fusion.7), kind=kCustom, calls=%fused_computation | custom fusion | bytes 4198400 | tf_op jit(solution)/shard_map/gather | solution.py:50
  92.4 14.6 %fusion.11 = bf16[1024,1024]{1,0:T(8,128)(2,1)} fusion(bf16[1,1024,1024]{2,1,0:T(8,128)(2,1)} %param.10, bf16[1024,1024]{1,0:T(8,128)(2,1)} %param.14, f32[1024,1024]{1,0:T(8,128)} %fusion.29, bf16[1024,1024]{1,0:T(8,128)(2,1)} %param.13, bf16[1024,1024]{1,0:T(8,128)(2,1)} %gather_fusion.7, bf16[1024,1024]{1,0:T(8,128)(2,1)} %gather_fusion.6, ...), kind=kOutput, calls=%fused_computation.23 | convolution fusion | flops 4326424576 | bytes 29360128 | tf_op jit(solution)/shard_map/dot_general | solution.py:57
  107.0 3.1 %fusion.30 = f32[1024,100]{0,1:T(8,128)} fusion(bf16[1024,1024]{1,0:T(8,128)(2,1)} %fusion.11, bf16[100,1024]{1,0:T(8,128)(2,1)S(1)} %copy-done.4), kind=kOutput, calls=%fused_computation.61 | convolution fusion | flops 209715200 | bytes 2711552 | tf_op jit(solution)/shard_map/dot_general | solution.py:59
  110.1 0.0 all-gather.4.cloned.1.call-update
  110.1 0.0 all-reduce.2.cloned.1.call-start
  110.2 33.8 %all-gather.4.cloned.1.call-done = f32[8,100,1024]{2,1,0:T(8,128)} async-done(((f32[1,100,1024]{2,1,0:T(8,128)}), f32[8,100,1024]{2,1,0:T(8,128)}) %all-gather.4.cloned.1.call-update) | async-done | bytes 3276816 | tf_op jit(solution)/shard_map/all_gather | solution.py:66
  144.0 2.9 %multiply_reduce_fusion = f32[100,1024]{1,0:T(8,128)S(1)} fusion(f32[8,100,1024]{2,1,0:T(8,128)} %all-gather.4.cloned.1.call-done, f32[100,1024]{1,0:T(8,128)} %bitcast.30), kind=kLoop, calls=%fused_computation.25 | loop fusion | flops 3993600 | bytes 4096000 | tf_op jit(solution)/shard_map/reduce_sum | solution.py:67
  146.9 0.1 multiply_convert_fusion.6
  147.1 1.2 fusion.31
  148.3 0.0 all-reduce.2.cloned.1.call-update
  148.3 2.1 convert_bitcast_fusion
  150.4 125.3 %all-reduce.2.cloned.1.call-done = f32[100,1024]{1,0:T(8,128)} async-done(((f32[100,1024]{1,0:T(8,128)}), f32[100,1024]{1,0:T(8,128)}) %all-reduce.2.cloned.1.call-update) | async-done | bytes 409616 | tf_op jit(solution)/shard_map/psum | solution.py:84
  275.6 1.8 broadcast_multiply_fusion
  (27 shorter events, 0.2 us)
Async XLA Ops:
  7.2 10.1 %copy-start = (bf16[1024,1024]{1,0:T(8,128)(2,1)S(1)}, bf16[1024,1024]{1,0:T(8,128)(2,1)}, u32[]{:S(2)}) copy-start(bf16[1024,1024]{1,0:T(8,128)(2,1)} %param.12) | copy-start | bytes 6291460
  7.2 136.8 %all-gather.4.cloned.1.call-start = ((), (), s32[]{:S(2)}) async-start(), calls=%async_computation.1 | async-start | bytes 3833856 | tf_op jit(solution)/shard_map/all_gather | solution.py:66
  7.2 3.0 %copy-start.1 = (bf16[1,1024,1024]{2,1,0:T(8,128)(2,1)S(1)}, bf16[1,1024,1024]{2,1,0:T(8,128)(2,1)}, u32[]{:S(2)}) copy-start(bf16[1,1024,1024]{2,1,0:T(8,128)(2,1)} %param.10) | copy-start | bytes 6291460
  10.3 6.9 %copy-start.6 = (s32[1024,8]{0,1:T(8,128)S(1)}, s32[1024,8]{0,1:T(8,128)}, u32[]{:S(2)}) copy-start(s32[1024,8]{0,1:T(8,128)} %param.16) | copy-start | bytes 98308
  10.9 10.7 %collective-permute-start = (bf16[128,1024]{1,0:T(8,128)(2,1)S(1)}, bf16[128,1024]{1,0:T(8,128)(2,1)S(1)}, u32[]{:S(2)}, u32[]{:S(2)}) collective-permute-start(bf16[128,1024]{1,0:T(8,128)(2,1)S(1)} %get-tuple-element.2), channel_id=1, source_target_pairs={{0,1},{1,2},{2,3},{4,5},{5,6},{6,7},{8,9},{9,10},{10,11},{12,13},{... | collective-permute-start | bytes 786440 | tf_op jit(solution)/shard_map/ppermute | solution.py:19
  15.8 9.7 %collective-permute-start.1 = (bf16[128,1024]{1,0:T(8,128)(2,1)S(1)}, bf16[128,1024]{1,0:T(8,128)(2,1)S(1)}, u32[]{:S(2)}, u32[]{:S(2)}) collective-permute-start(bf16[128,1024]{1,0:T(8,128)(2,1)S(1)} %get-tuple-element.3), channel_id=1, source_target_pairs={{1,0},{2,1},{3,2},{5,4},{6,5},{7,6},{9,8},{10,9},{11,10},{13,12},{... | collective-permute-start | bytes 786440 | tf_op jit(solution)/shard_map/ppermute | solution.py:22
  92.4 14.6 %copy-start.4 = (bf16[100,1024]{1,0:T(8,128)(2,1)S(1)}, bf16[100,1024]{1,0:T(8,128)(2,1)}, u32[]{:S(2)}) copy-start(bf16[100,1024]{1,0:T(8,128)(2,1)} %param.15) | copy-start | bytes 614404
  110.1 165.5 %all-reduce.2.cloned.1.call-start = ((), (), s32[]{:S(2)}) async-start(), calls=%async_computation | async-start | bytes 851968 | tf_op jit(solution)/shard_map/psum | solution.py:84
  143.9 2.9 %copy-start.3 = (f32[1024,100]{0,1:T(8,128)S(1)}, f32[1024,100]{0,1:T(8,128)}, u32[]{:S(2)}) copy-start(f32[1024,100]{0,1:T(8,128)} %fusion.30) | copy-start | bytes 1228804
  143.9 2.9 %copy-start.5 = (f32[100,1024]{1,0:T(8,128)S(1)}, f32[100,1024]{1,0:T(8,128)}, u32[]{:S(2)}) copy-start(f32[100,1024]{1,0:T(8,128)} %param.17) | copy-start | bytes 1228804
  143.9 2.9 %copy-start.7 = (f32[1024]{0:T(1024)S(1)}, f32[1024]{0:T(1024)}, u32[]{:S(2)}) copy-start(f32[1024]{0:T(1024)} %param.19) | copy-start | bytes 12292
  143.9 3.0 %copy-start.8 = (f32[100]{0:T(128)S(1)}, f32[100]{0:T(128)}, u32[]{:S(2)}) copy-start(f32[100]{0:T(128)} %param.18) | copy-start | bytes 1204
  143.9 3.1 %copy-start.2 = (bf16[1024,1024]{1,0:T(8,128)(2,1)S(1)}, bf16[1024,1024]{1,0:T(8,128)(2,1)}, u32[]{:S(2)}) copy-start(bf16[1024,1024]{1,0:T(8,128)(2,1)} %fusion.11) | copy-start | bytes 6291460
Sparse Core Ops, SparseCore 0:
  110.3 33.6 all-gather.3
  149.8 125.7 all-reduce.1
where the time goes:
time: 285 us; the launch traced here: 284 us
  waiting for transfers between devices  163 us (57%)
  local copies, waits for them, and re-layouts  65.2 us (23%)
  matrix products  25.3 us (9%)
  between operations  14.3 us (5%)
  other arithmetic  10.3 us (4%)
  starting transfers between devices  6.32 us (2%)
    psum x1, waiting for transfers between devices, local(): total_decoder = lax.psum(local_decoder, ('member', 'space'))  125 us
    gather x8, local copies, waits for them, and re-layouts, local(): summed = summed + extended[edge_index[:, column]].astype(jnp.float32)  65.1 us
    all_gather x1, waiting for transfers between devices, local(): lax.all_gather(prediction_field[None], 'member', axis=0, tiled=True)  33.8 us
    dot_general x1, matrix products, local(): jnp.dot(activated, w_out, preferred_element_type=jnp.float32)  14.6 us
  transfers between devices with their start and end apart: 4, of which 3 were waited for; matrix products, arithmetic and copies ran while one was open for 2% of the time, Pallas kernels for 0%

commit v1 on v0

v1 whole, which is shorter than its diff:
```python
import functools
import math

import jax
import jax.numpy as jnp
from jax import lax
from jax.experimental import pallas as pl
from jax.experimental.pallas import tpu as pltpu
from jax.sharding import PartitionSpec as P

HALO = 128
TAU = 0.05
ALPHA = 0.95
BLOCK = 256
LANES = 128
MESH = pl.DeviceIdType.MESH


def soft(diff):
    return diff * lax.rsqrt(diff * diff + TAU * TAU)


def gelu(x):
    return 0.5 * x * (1.0 + jnp.tanh(math.sqrt(2.0 / math.pi) * (x + 0.044715 * (x * x * x))))


def kernel(
    members,
    spaces,
    x_hbm,
    gain_ref,
    ws_hbm,
    wn_hbm,
    wo_hbm,
    readout_ref,
    edge_ref,
    truth_ref,
    var_ref,
    area_ref,
    grads_out,
    decoder_out,
    x_ref,
    ws_ref,
    wn_ref,
    wo_ref,
    ext_ref,
    hidden_ref,
    wide_ref,
    read_ref,
    truth_t,
    var_pad,
    f_ref,
    fr_ref,
    gs_ref,
    g_ref,
    d_ref,
    ds_ref,
    dr_ref,
    z_ref,
    ag_ref,
    load_sem,
    halo_send,
    halo_recv,
    f_send,
    f_recv,
    g_send,
    g_recv,
    d_send,
    d_recv,
    z_send,
    z_recv,
    ag_send,
    ag_recv,
):
    me = lax.axis_index("member")
    sp = lax.axis_index("space")
    nodes, width = x_ref.shape
    variables = readout_ref.shape[0]
    blocks = nodes // BLOCK
    part = BLOCK // members
    rows = width // members

    def load(src, dst, sem):
        return pltpu.make_async_copy(src, dst, load_sem.at[sem])

    x_parts = ((0, HALO), (nodes - HALO, HALO), (HALO, nodes - 2 * HALO))
    loads = [load(x_hbm.at[pl.ds(a, n)], x_ref.at[pl.ds(a, n)], i) for i, (a, n) in enumerate(x_parts)]
    loads += [load(ws_hbm, ws_ref, 3), load(wn_hbm, wn_ref, 4), load(wo_hbm, wo_ref, 5)]
    for item in loads:
        item.start()

    barrier = pltpu.get_barrier_semaphore()
    for d in range(1, members):
        pl.semaphore_signal(barrier, inc=1, device_id={"member": lax.rem(me + d, members)}, device_id_type=MESH)
    for d in range(1, spaces):
        pl.semaphore_signal(barrier, inc=1, device_id={"space": lax.rem(sp + d, spaces)}, device_id_type=MESH)

    gain = gain_ref[...].astype(jnp.float32)

    def norm(start, count):
        values = x_ref[pl.ds(start, count), :].astype(jnp.float32)
        scale = lax.rsqrt(jnp.mean(values * values, axis=-1, keepdims=True) + 1e-06)
        ext_ref[pl.ds(start + HALO, count), :] = (values * scale * gain).astype(jnp.bfloat16)

    loads[0].wait()
    norm(0, HALO)
    loads[1].wait()
    norm(nodes - HALO, HALO)

    pl.semaphore_wait(barrier, members - 1 + spaces - 1)

    down = pltpu.make_async_remote_copy(
        src_ref=ext_ref.at[pl.ds(HALO, HALO)],
        dst_ref=ext_ref.at[pl.ds(nodes + HALO, HALO)],
        send_sem=halo_send.at[0],
        recv_sem=halo_recv.at[0],
        device_id={"space": jnp.maximum(sp - 1, 0)},
        device_id_type=MESH,
    )
    up = pltpu.make_async_remote_copy(
        src_ref=ext_ref.at[pl.ds(nodes, HALO)],
        dst_ref=ext_ref.at[pl.ds(0, HALO)],
        send_sem=halo_send.at[1],
        recv_sem=halo_recv.at[1],
        device_id={"space": jnp.minimum(sp + 1, spaces - 1)},
        device_id_type=MESH,
    )

    @pl.when(sp > 0)
    def _():
        down.start()

    @pl.when(sp < spaces - 1)
    def _():
        up.start()

    @pl.when(sp == 0)
    def _():
        ext_ref[pl.ds(0, HALO), :] = jnp.zeros((HALO, width), jnp.bfloat16)

    @pl.when(sp == spaces - 1)
    def _():
        ext_ref[pl.ds(nodes + HALO, HALO), :] = jnp.zeros((HALO, width), jnp.bfloat16)

    loads[2].wait()
    lax.fori_loop(1, nodes // HALO - 1, lambda i, _: (norm(pl.multiple_of(i * HALO, HALO), HALO), 0)[1], 0)

    wide_ref[...] = jnp.zeros_like(wide_ref)
    wide_ref[pl.ds(0, variables), :] = readout_ref[...].astype(jnp.float32)
    read_ref[...] = wide_ref[...].astype(jnp.bfloat16)
    wide2 = d_ref
    wide2[...] = jnp.zeros_like(wide2)
    wide2[pl.ds(0, variables), pl.ds(0, nodes)] = truth_ref[...]
    wide2[pl.ds(variables, 1), pl.ds(0, nodes)] = area_ref[...]
    for j in range(nodes // LANES):
        at = j * LANES
        tile = wide2[:, pl.ds(at, LANES)].T
        per = LANES // part
        block, owner = at // BLOCK, (at % BLOCK) // part
        for k in range(per):
            truth_t[block, owner + k] = tile[k * part : (k + 1) * part, :]
    var_pad[...] = jnp.zeros_like(var_pad)
    var_pad[pl.ds(0, 1), pl.ds(0, variables)] = var_ref[...]
    d_ref[...] = jnp.zeros_like(d_ref)

    for item in loads[3:]:
        item.wait()

    def f_copy(b, d):
        return pltpu.make_async_remote_copy(
            src_ref=f_ref.at[b, lax.rem(me + d, members)],
            dst_ref=fr_ref.at[b, d],
            send_sem=f_send.at[b, d],
            recv_sem=f_recv.at[b, d],
            device_id={"member": lax.rem(me + d, members)},
            device_id_type=MESH,
        )

    def g_copy(b, d):
        return pltpu.make_async_remote_copy(
            src_ref=gs_ref.at[b, d],
            dst_ref=g_ref.at[b, me],
            send_sem=g_send.at[b, d],
            recv_sem=g_recv.at[b, d],
            device_id={"member": lax.rem(me + members - d, members)},
            device_id_type=MESH,
        )

    def advance(b):
        start = pl.multiple_of(b * BLOCK, BLOCK)
        local = edge_ref[pl.ds(start, BLOCK), :] - start
        columns = lax.broadcasted_iota(jnp.int32, (BLOCK, BLOCK + 2 * HALO), 1)
        count = jnp.zeros((BLOCK, BLOCK + 2 * HALO), jnp.float32)
        for k in range(edge_ref.shape[1]):
            count = count + jnp.where(local[:, k : k + 1] == columns, 1.0, 0.0)
        near = ext_ref[pl.ds(start, BLOCK + 2 * HALO), :]
        mean = jnp.dot(count.astype(jnp.bfloat16), near, preferred_element_type=jnp.float32)
        mean = (mean * (1.0 / edge_ref.shape[1])).astype(jnp.bfloat16)
        own = ext_ref[pl.ds(start + HALO, BLOCK), :]
        inside = jnp.dot(own, ws_ref[...], preferred_element_type=jnp.float32) + jnp.dot(
            mean, wn_ref[...], preferred_element_type=jnp.float32
        )
        activated = gelu(inside).astype(jnp.bfloat16)
        update = jnp.dot(activated, wo_ref[...], preferred_element_type=jnp.float32)
        hidden = (x_ref[pl.ds(start, BLOCK), :].astype(jnp.float32) + update).astype(jnp.bfloat16)
        hidden_ref[pl.ds(start, BLOCK), :] = hidden
        forecast = lax.dot_general(
            hidden, read_ref[...], (((1,), (1,)), ((), ())), preferred_element_type=jnp.float32
        )
        f_ref[b] = forecast.reshape(members, part, LANES)
        for d in range(1, members):
            f_copy(b, d).start()

    eps = (1.0 - ALPHA) / members
    couple = (1.0 - eps) / (members - 1)

    def score(b):
        for d in range(1, members):
            f_copy(b, d).wait_recv()
        truth = truth_t[b, me]
        weight = var_pad[pl.ds(0, 1), :] * truth[:, variables : variables + 1]
        values = [f_ref[b, me]] + [fr_ref[b, d] for d in range(1, members)]
        spread = [jnp.zeros((part, LANES), jnp.float32) for _ in range(members)]
        for i in range(members):
            for j in range(i + 1, members):
                sign = soft(values[i] - values[j])
                spread[i] = spread[i] + sign
                spread[j] = spread[j] - sign
        for d in range(members):
            grad = (weight * (soft(values[d] - truth) - couple * spread[d])).astype(jnp.bfloat16)
            if d == 0:
                g_ref[b, me] = grad
            else:
                gs_ref[b, d] = grad
                g_copy(b, d).start()

    def collect(b):
        start = pl.multiple_of(b * BLOCK, BLOCK)
        for d in range(1, members):
            g_copy(b, d).wait_recv()
        grads = g_ref[b].reshape(BLOCK, LANES)
        grads_out[pl.ds(start, BLOCK), :] = grads
        d_ref[...] += lax.dot_general(
            grads,
            hidden_ref[pl.ds(start, BLOCK), :],
            (((0,), (0,)), ((), ())),
            preferred_element_type=jnp.float32,
        )

    def order(i):
        return lax.rem(i + 1, blocks)

    def step(i, carry):
        @pl.when(i == blocks - 2)
        def _():
            @pl.when(sp > 0)
            def _():
                up.wait_recv()

            @pl.when(sp < spaces - 1)
            def _():
                down.wait_recv()

        advance(order(i))

        @pl.when(i >= 1)
        def _():
            score(order(i - 1))

        @pl.when(i >= 2)
        def _():
            collect(order(i - 2))

        return carry

    lax.fori_loop(0, blocks, step, 0)
    score(order(blocks - 1))
    collect(order(blocks - 2))
    collect(order(blocks - 1))

    ds_ref[...] = d_ref[...].T.reshape(members, rows, LANES).astype(jnp.bfloat16)

    def d_copy(d):
        return pltpu.make_async_remote_copy(
            src_ref=ds_ref.at[lax.rem(me + d, members)],
            dst_ref=dr_ref.at[d],
            send_sem=d_send.at[d],
            recv_sem=d_recv.at[d],
            device_id={"member": lax.rem(me + d, members)},
            device_id_type=MESH,
        )

    def z_copy(d):
        return pltpu.make_async_remote_copy(
            src_ref=z_ref.at[sp],
            dst_ref=z_ref.at[sp],
            send_sem=z_send.at[d],
            recv_sem=z_recv.at[d],
            device_id={"space": lax.rem(sp + d, spaces)},
            device_id_type=MESH,
        )

    def ag_copy(d):
        return pltpu.make_async_remote_copy(
            src_ref=ag_ref.at[me],
            dst_ref=ag_ref.at[me],
            send_sem=ag_send.at[d],
            recv_sem=ag_recv.at[d],
            device_id={"member": lax.rem(me + d, members)},
            device_id_type=MESH,
        )

    for d in range(1, members):
        d_copy(d).start()
    total = ds_ref[me].astype(jnp.float32)
    for d in range(1, members):
        d_copy(d).wait_recv()
        total = total + dr_ref[d].astype(jnp.float32)
    z_ref[sp] = total.astype(jnp.bfloat16)
    for d in range(1, spaces):
        z_copy(d).start()
    for d in range(1, spaces):
        z_copy(d).wait_recv()
    total = z_ref[0].astype(jnp.float32)
    for s in range(1, spaces):
        total = total + z_ref[s].astype(jnp.float32)
    ag_ref[me] = (total / math.sqrt(members * nodes * spaces)).astype(jnp.bfloat16)
    for d in range(1, members):
        ag_copy(d).start()
    for d in range(1, members):
        ag_copy(d).wait_recv()
    decoder_out[...] = ag_ref[...].reshape(width, LANES)

    @pl.when(sp > 0)
    def _():
        down.wait_send()

    @pl.when(sp < spaces - 1)
    def _():
        up.wait_send()

    def drain(b, carry):
        for d in range(1, members):
            f_copy(b, d).wait_send()
            g_copy(b, d).wait_send()
        return carry

    lax.fori_loop(0, blocks, drain, 0)
    for d in range(1, members):
        d_copy(d).wait_send()
        ag_copy(d).wait_send()
    for d in range(1, spaces):
        z_copy(d).wait_send()


def local(
    realization_channels,
    node_gain,
    w_self,
    w_neighbour,
    w_out,
    readout_map,
    edge_index,
    verifying_truth,
    var_weight,
    area_weight,
):
    members, spaces = lax.axis_size("member"), lax.axis_size("space")
    x = realization_channels[0]
    nodes, width = x.shape
    variables = readout_map.shape[0]
    blocks, part, rows = nodes // BLOCK, BLOCK // members, width // members
    bf16, f32 = jnp.bfloat16, jnp.float32
    dma = pltpu.SemaphoreType.DMA
    hbm, vmem = pl.BlockSpec(memory_space=pl.ANY), pl.BlockSpec(memory_space=pltpu.VMEM)
    grads, decoder = pl.pallas_call(
        functools.partial(kernel, members, spaces),
        out_shape=(
            jax.ShapeDtypeStruct((nodes, LANES), bf16),
            jax.ShapeDtypeStruct((width, LANES), bf16),
        ),
        in_specs=[hbm, vmem, hbm, hbm, hbm, vmem, vmem, vmem, vmem, vmem],
        out_specs=(vmem, vmem),
        scratch_shapes=[
            pltpu.VMEM((nodes, width), bf16),
            pltpu.VMEM((width, width), bf16),
            pltpu.VMEM((width, width), bf16),
            pltpu.VMEM((width, width), bf16),
            pltpu.VMEM((nodes + 2 * HALO, width), bf16),
            pltpu.VMEM((nodes, width), bf16),
            pltpu.VMEM((LANES, width), f32),
            pltpu.VMEM((LANES, width), bf16),
            pltpu.VMEM((blocks, members, part, LANES), f32),
            pltpu.VMEM((8, LANES), f32),
            pltpu.VMEM((blocks, members, part, LANES), f32),
            pltpu.VMEM((blocks, members, part, LANES), f32),
            pltpu.VMEM((blocks, members, part, LANES), bf16),
            pltpu.VMEM((blocks, members, part, LANES), bf16),
            pltpu.VMEM((LANES, max(width, nodes)), f32),
            pltpu.VMEM((members, rows, LANES), bf16),
            pltpu.VMEM((members, rows, LANES), bf16),
            pltpu.VMEM((spaces, rows, LANES), bf16),
            pltpu.VMEM((members, rows, LANES), bf16),
            dma((6,)),
            dma((2,)),
            dma((2,)),
            dma((blocks, members)),
            dma((blocks, members)),
            dma((blocks, members)),
            dma((blocks, members)),
            dma((members,)),
            dma((members,)),
            dma((spaces,)),
            dma((spaces,)),
            dma((members,)),
            dma((members,)),
        ],
        compiler_params=pltpu.CompilerParams(
            collective_id=0, has_side_effects=True, vmem_limit_bytes=48 * 2**20
        ),
    )(
        x,
        node_gain[None],
        w_self,
        w_neighbour,
        w_out,
        readout_map,
        edge_index,
        verifying_truth,
        var_weight[None],
        area_weight[None],
    )
    grad_hidden = jnp.dot(grads[:, :variables], readout_map, preferred_element_type=f32).astype(bf16)
    grad_decoder = decoder[:, :variables].T.astype(f32)
    return grad_hidden[None], grad_decoder


def solution(mesh):
    return jax.shard_map(
        local,
        mesh=mesh,
        in_specs=(
            P("member", "space", None),
            P(),
            P(),
            P(),
            P(),
            P(),
            P("space", None),
            P(None, "space"),
            P(),
            P("space"),
        ),
        out_specs=(P("member", "space", None), P()),
        check_vma=False,
    )
```

time: 285 us -> 54.4 us (0.19)
  waiting for transfers between devices: 163 us -> 0 us
  local copies, waits for them, and re-layouts: 65.2 us -> 9.07 us
  Pallas kernels: 0 us -> 42.2 us
  matrix products: 25.3 us -> 2.01 us
  between operations: 14.3 us -> 0.67 us
  other arithmetic: 10.3 us -> 0.04 us
  starting transfers between devices: 6.32 us -> 0 us
    psum x1 -> x0, waiting for transfers between devices: 125 us -> none  [local(): total_decoder = lax.psum(local_decoder, ('member', 'space'))]
    gather x8 -> x0, local copies, waits for them, and re-layouts: 65.1 us -> none  [local(): summed = summed + extended[edge_index[:, column]].astype(jnp.float32)]
    pallas_call x0 -> x1, Pallas kernels: none -> 42.2 us  [local(): pl.pallas_call(functools.partial(kernel, members, spaces), out_shape=(jax...]
    all_gather x1 -> x0, waiting for transfers between devices: 33.8 us -> none  [local(): lax.all_gather(prediction_field[None], 'member', axis=0, tiled=True)]
    dot_general x5 -> x1, matrix products: 25.3 us -> 2.01 us  [local(): jnp.dot(grads[:, :variables], readout_map, preferred_element_type=f32)]
    unnamed x18 -> x16, local copies, waits for them, and re-layouts: 0.04 us -> 8.39 us
    ppermute x2 -> x0, starting transfers between devices: 6.24 us -> none  [the longest x1 4.94 us: padded(): lax.ppermute(lax.slice_in_dim(block, block.shape[dim] - width, None, axis...]
    reduce_sum x2 -> x0, other arithmetic: 5.07 us -> none  [the longest x1 2.91 us: local(): jnp.sum(softened_sign(prediction_field[None] - entire_collection), axis=0)]
  transfers between devices with their start and end apart: 4 -> 0, of which waited for: 3 -> 0; matrix products, arithmetic and copies ran while one was open for 2% -> 0% of each run, Pallas kernels for 0% -> 0%
where the time goes in v1:
time: 54.4 us; the launch traced here: 54 us
  Pallas kernels  42.2 us (78%)
  local copies, waits for them, and re-layouts  9.07 us (17%)
  matrix products  2.01 us (4%)
  between operations  0.67 us (1%)
    pallas_call x1, Pallas kernels, local(): pl.pallas_call(functools.partial(kernel, members, spaces), out_shape=(jax...  42.2 us
    unnamed x16, local copies, waits for them, and re-layouts  8.39 us
    dot_general x1, matrix products, local(): jnp.dot(grads[:, :variables], readout_map, preferred_element_type=f32)  2.01 us

profile of v1, /device:TPU:0, one launch (start us, length us, event | category | flops | bytes accessed | tf_op | source)
XLA Modules:
  0.0 54.0 jit_solution(14485677770203834591)
XLA Ops:
  0.6 0.7 %broadcast_in_dim.12.gain_ref = bf16[1,1024]{1,0:T(2,128)(2,1)S(1)} reshape(bf16[1024]{0:T(1024)(128)(2,1)} %param.11) | data formatting | bytes 4096 | tf_op jit(solution)/shard_map/broadcast_in_dim | solution.py:423
  1.3 0.9 %copy.12.edge_ref = s32[1024,8]{1,0:T(8,128)S(1)} copy(s32[1024,8]{0,1:T(8,128)} %param.16) | data formatting | bytes 65536 | tf_op args[6]
  2.3 0.0 copy-start
  2.3 1.6 %copy-done = bf16[1,1024,1024]{2,1,0:T(8,128)(2,1)S(1)} copy-done((bf16[1,1024,1024]{2,1,0:T(8,128)(2,1)S(1)}, bf16[1,1024,1024]{2,1,0:T(8,128)(2,1)}, u32[]{:S(2)}) %copy-start) | copy-done | bytes 2097176
  3.9 0.0 copy-start.1
  3.9 1.6 %copy-done.1 = bf16[1024,1024]{1,0:T(8,128)(2,1)S(1)} copy-done((bf16[1024,1024]{1,0:T(8,128)(2,1)S(1)}, bf16[1024,1024]{1,0:T(8,128)(2,1)}, u32[]{:S(2)}) %copy-start.1) | copy-done | bytes 2097176
  5.5 0.0 copy-start.2
  5.5 0.9 %copy-done.2 = bf16[100,1024]{1,0:T(8,128)(2,1)S(1)} copy-done((bf16[100,1024]{1,0:T(8,128)(2,1)S(1)}, bf16[100,1024]{1,0:T(8,128)(2,1)}, u32[]{:S(2)}) %copy-start.2) | copy-done | bytes 204824
  6.4 0.0 copy-start.4
  6.4 1.0 %copy-done.4 = f32[100,1024]{1,0:T(8,128)S(1)} copy-done((f32[100,1024]{1,0:T(8,128)S(1)}, f32[100,1024]{1,0:T(8,128)}, u32[]{:S(2)}) %copy-start.4) | copy-done | bytes 409624
  7.4 0.0 copy-start.5
  7.4 0.7 %copy-done.5 = f32[1024]{0:T(1024)S(1)} copy-done((f32[1024]{0:T(1024)S(1)}, f32[1024]{0:T(1024)}, u32[]{:S(2)}) %copy-start.5) | copy-done | bytes 4120
  8.1 0.0 copy-start.6
  8.1 0.7 %copy-done.6 = f32[100]{0:T(128)S(1)} copy-done((f32[100]{0:T(128)S(1)}, f32[100]{0:T(128)}, u32[]{:S(2)}) %copy-start.6) | copy-done | bytes 424
  8.7 0.0 copy-start.3
  8.7 42.2 %shard_map.113 = (bf16[1024,128]{1,0:T(8,128)(2,1)S(1)}, bf16[1024,128]{1,0:T(8,128)(2,1)S(1)}) custom-call(bf16[1024,1024]{1,0:T(8,128)(2,1)S(1)} %bitcast.8, bf16[1,1024]{1,0:T(2,128)(2,1)S(1)} %broadcast_in_dim.12.gain_ref, bf16[1024,1024]{1,0:T(8,128)(2,1)S(1)} %copy-done.1, bf16[1024,1024]{1,0:T(8,128)(2,1)} %wn_hbm.1, bf16[1024,1024]{1,0:T(8,128)(2,1)} %wo_hbm.1, ...), custom_call_target="tpu_custom_call" | custom-call | tf_op jit(solution)/shard_map/pallas_call | solution.py:376
  51.0 1.0 %copy.13 = f32[100,1024]{1,0:T(8,128)} copy(f32[100,1024]{0,1:T(8,128)S(1)} %convert_bitcast_fusion.1) | data formatting | bytes 819200
  52.0 0.0 copy-done.3
  52.0 2.0 %convert_bitcast_fusion = bf16[1,1024,1024]{2,1,0:T(8,128)(2,1)} fusion(bf16[100,1024]{1,0:T(8,128)(2,1)S(1)} %copy-done.3, bf16[1024,128]{1,0:T(8,128)(2,1)S(1)} %get-tuple-element.4), kind=kOutput, calls=%fused_computation | convolution fusion | flops 210763776 | bytes 2564096 | tf_op jit(solution)/shard_map/dot_general | solution.py:433
  (1 shorter events, 0.0 us)
Async XLA Ops:
  2.3 1.6 %copy-start = (bf16[1,1024,1024]{2,1,0:T(8,128)(2,1)S(1)}, bf16[1,1024,1024]{2,1,0:T(8,128)(2,1)}, u32[]{:S(2)}) copy-start(bf16[1,1024,1024]{2,1,0:T(8,128)(2,1)} %param.10) | copy-start | bytes 6291460
  3.9 1.6 %copy-start.1 = (bf16[1024,1024]{1,0:T(8,128)(2,1)S(1)}, bf16[1024,1024]{1,0:T(8,128)(2,1)}, u32[]{:S(2)}) copy-start(bf16[1024,1024]{1,0:T(8,128)(2,1)} %ws_hbm.1) | copy-start | bytes 6291460
  5.5 0.9 %copy-start.2 = (bf16[100,1024]{1,0:T(8,128)(2,1)S(1)}, bf16[100,1024]{1,0:T(8,128)(2,1)}, u32[]{:S(2)}) copy-start(bf16[100,1024]{1,0:T(8,128)(2,1)} %readout_ref.1) | copy-start | bytes 614404
  6.4 1.0 %copy-start.4 = (f32[100,1024]{1,0:T(8,128)S(1)}, f32[100,1024]{1,0:T(8,128)}, u32[]{:S(2)}) copy-start(f32[100,1024]{1,0:T(8,128)} %truth_ref.1) | copy-start | bytes 1228804
  7.4 0.7 %copy-start.5 = (f32[1024]{0:T(1024)S(1)}, f32[1024]{0:T(1024)}, u32[]{:S(2)}) copy-start(f32[1024]{0:T(1024)} %param.19) | copy-start | bytes 12292
  8.1 0.7 %copy-start.6 = (f32[100]{0:T(128)S(1)}, f32[100]{0:T(128)}, u32[]{:S(2)}) copy-start(f32[100]{0:T(128)} %param.18) | copy-start | bytes 1204
  8.7 43.3 %copy-start.3 = (bf16[100,1024]{1,0:T(8,128)(2,1)S(1)}, bf16[100,1024]{1,0:T(8,128)(2,1)}, u32[]{:S(2)}) copy-start(bf16[100,1024]{1,0:T(8,128)(2,1)} %readout_ref.1) | copy-start | bytes 614404

commit v2 on v1

--- a/solution.py
+++ b/solution.py
@@ -28,18 +28,25 @@
     members,
     spaces,
     x_hbm,
-    gain_ref,
+    gain_hbm,
     ws_hbm,
     wn_hbm,
     wo_hbm,
+    readout_hbm,
+    edge_hbm,
+    truth_hbm,
+    var_hbm,
+    area_hbm,
+    grads_out,
+    decoder_out,
+    x_ref,
+    gain_ref,
     readout_ref,
+    edge_rows,
     edge_ref,
     truth_ref,
     var_ref,
     area_ref,
-    grads_out,
-    decoder_out,
-    x_ref,
     ws_ref,
     wn_ref,
     wo_ref,
@@ -86,7 +93,15 @@
     x_parts = ((0, HALO), (nodes - HALO, HALO), (HALO, nodes - 2 * HALO))
     loads = [load(x_hbm.at[pl.ds(a, n)], x_ref.at[pl.ds(a, n)], i) for i, (a, n) in enumerate(x_parts)]
     loads += [load(ws_hbm, ws_ref, 3), load(wn_hbm, wn_ref, 4), load(wo_hbm, wo_ref, 5)]
-    for item in loads:
+    small = [
+        load(gain_hbm, gain_ref, 6),
+        load(edge_hbm, edge_rows, 7),
+        load(readout_hbm, readout_ref, 8),
+        load(truth_hbm, truth_ref, 9),
+        load(var_hbm, var_ref, 10),
+        load(area_hbm, area_ref, 11),
+    ]
+    for item in small[:1] + loads[:3] + small[1:] + loads[3:]:
         item.start()
 
     barrier = pltpu.get_barrier_semaphore()
@@ -95,7 +110,8 @@
     for d in range(1, spaces):
         pl.semaphore_signal(barrier, inc=1, device_id={"space": lax.rem(sp + d, spaces)}, device_id_type=MESH)
 
-    gain = gain_ref[...].astype(jnp.float32)
+    small[0].wait()
+    gain = gain_ref[...].astype(jnp.float32)[None, :]
 
     def norm(start, count):
         values = x_ref[pl.ds(start, count), :].astype(jnp.float32)
@@ -145,13 +161,16 @@
     loads[2].wait()
     lax.fori_loop(1, nodes // HALO - 1, lambda i, _: (norm(pl.multiple_of(i * HALO, HALO), HALO), 0)[1], 0)
 
+    for item in small[1:]:
+        item.wait()
+    edge_ref[...] = edge_rows[...].T
     wide_ref[...] = jnp.zeros_like(wide_ref)
     wide_ref[pl.ds(0, variables), :] = readout_ref[...].astype(jnp.float32)
     read_ref[...] = wide_ref[...].astype(jnp.bfloat16)
     wide2 = d_ref
     wide2[...] = jnp.zeros_like(wide2)
     wide2[pl.ds(0, variables), pl.ds(0, nodes)] = truth_ref[...]
-    wide2[pl.ds(variables, 1), pl.ds(0, nodes)] = area_ref[...]
+    wide2[pl.ds(variables, 1), pl.ds(0, nodes)] = area_ref[...][None, :]
     for j in range(nodes // LANES):
         at = j * LANES
         tile = wide2[:, pl.ds(at, LANES)].T
@@ -160,7 +179,7 @@
         for k in range(per):
             truth_t[block, owner + k] = tile[k * part : (k + 1) * part, :]
     var_pad[...] = jnp.zeros_like(var_pad)
-    var_pad[pl.ds(0, 1), pl.ds(0, variables)] = var_ref[...]
+    var_pad[pl.ds(0, 1), pl.ds(0, variables)] = var_ref[...][None, :]
     d_ref[...] = jnp.zeros_like(d_ref)
 
     for item in loads[3:]:
@@ -372,17 +391,24 @@
     blocks, part, rows = nodes // BLOCK, BLOCK // members, width // members
     bf16, f32 = jnp.bfloat16, jnp.float32
     dma = pltpu.SemaphoreType.DMA
-    hbm, vmem = pl.BlockSpec(memory_space=pl.ANY), pl.BlockSpec(memory_space=pltpu.VMEM)
+    hbm, vmem = pl.BlockSpec(memory_space=pltpu.HBM), pl.BlockSpec(memory_space=pltpu.VMEM)
     grads, decoder = pl.pallas_call(
         functools.partial(kernel, members, spaces),
         out_shape=(
-            jax.ShapeDtypeStruct((nodes, LANES), bf16),
-            jax.ShapeDtypeStruct((width, LANES), bf16),
+            pltpu.VMEM((nodes, LANES), bf16),
+            pltpu.VMEM((width, LANES), bf16),
         ),
-        in_specs=[hbm, vmem, hbm, hbm, hbm, vmem, vmem, vmem, vmem, vmem],
+        in_specs=[hbm] * 10,
         out_specs=(vmem, vmem),
         scratch_shapes=[
             pltpu.VMEM((nodes, width), bf16),
+            pltpu.VMEM((width,), bf16),
+            pltpu.VMEM((variables, width), bf16),
+            pltpu.VMEM(edge_index.shape[::-1], jnp.int32),
+            pltpu.VMEM(edge_index.shape, jnp.int32),
+            pltpu.VMEM((variables, nodes), f32),
+            pltpu.VMEM((variables,), f32),
+            pltpu.VMEM((nodes,), f32),
             pltpu.VMEM((width, width), bf16),
             pltpu.VMEM((width, width), bf16),
             pltpu.VMEM((width, width), bf16),
@@ -401,7 +427,7 @@
             pltpu.VMEM((members, rows, LANES), bf16),
             pltpu.VMEM((spaces, rows, LANES), bf16),
             pltpu.VMEM((members, rows, LANES), bf16),
-            dma((6,)),
+            dma((12,)),
             dma((2,)),
             dma((2,)),
             dma((blocks, members)),
@@ -416,19 +442,19 @@
             dma((members,)),
         ],
         compiler_params=pltpu.CompilerParams(
-            collective_id=0, has_side_effects=True, vmem_limit_bytes=48 * 2**20
+            collective_id=0, has_side_effects=True, vmem_limit_bytes=61 * 2**20
         ),
     )(
         x,
-        node_gain[None],
+        node_gain,
         w_self,
         w_neighbour,
         w_out,
         readout_map,
-        edge_index,
+        edge_index.T,
         verifying_truth,
-        var_weight[None],
-        area_weight[None],
+        var_weight,
+        area_weight,
     )
     grad_hidden = jnp.dot(grads[:, :variables], readout_map, preferred_element_type=f32).astype(bf16)
     grad_decoder = decoder[:, :variables].T.astype(f32)

time: 54.4 us -> 46.4 us (0.85)
  local copies, waits for them, and re-layouts: 9.07 us -> 0.98 us
    unnamed x16 -> x3, local copies, waits for them, and re-layouts: 8.39 us -> 0.98 us
    broadcast_in_dim x1 -> x0, local copies, waits for them, and re-layouts: 0.69 us -> none  [local(): node_gain[None]]
where the time goes in v2:
time: 46.4 us; the launch traced here: 46.2 us
  Pallas kernels  42.5 us (92%)
  matrix products  2.01 us (4%)
  local copies, waits for them, and re-layouts  0.98 us (2%)
  between operations  0.66 us (1%)
    pallas_call x1, Pallas kernels, local(): pl.pallas_call(functools.partial(kernel, members, spaces), out_shape=(plt...  42.5 us
    dot_general x1, matrix products, local(): jnp.dot(grads[:, :variables], readout_map, preferred_element_type=f32)  2.01 us
    unnamed x3, local copies, waits for them, and re-layouts  0.98 us

profile of v2, /device:TPU:0, one launch (start us, length us, event | category | flops | bytes accessed | tf_op | source)
XLA Modules:
  0.0 46.2 jit_solution(5900542619904821276)
XLA Ops:
  0.6 0.0 copy-start
  0.6 42.5 %shard_map.113 = (bf16[1024,128]{1,0:T(8,128)(2,1)S(1)}, bf16[1024,128]{1,0:T(8,128)(2,1)S(1)}) custom-call(bf16[1024,1024]{1,0:T(8,128)(2,1)} %bitcast.7, bf16[1024]{0:T(1024)(128)(2,1)} %gain_hbm.1, bf16[1024,1024]{1,0:T(8,128)(2,1)} %ws_hbm.1, bf16[1024,1024]{1,0:T(8,128)(2,1)} %wn_hbm.1, bf16[1024,1024]{1,0:T(8,128)(2,1)} %wo_hbm.1, ...), custom_call_target="tpu_custom_call" | custom-call | tf_op jit(solution)/shard_map/pallas_call | solution.py:395
  43.2 1.0 %copy.12 = f32[100,1024]{1,0:T(8,128)} copy(f32[100,1024]{0,1:T(8,128)S(1)} %convert_bitcast_fusion.1) | data formatting | bytes 819200
  44.2 0.0 copy-done
  44.2 2.0 %convert_bitcast_fusion = bf16[1,1024,1024]{2,1,0:T(8,128)(2,1)} fusion(bf16[100,1024]{1,0:T(8,128)(2,1)S(1)} %copy-done, bf16[1024,128]{1,0:T(8,128)(2,1)S(1)} %get-tuple-element.4), kind=kOutput, calls=%fused_computation | convolution fusion | flops 210763776 | bytes 2564096 | tf_op jit(solution)/shard_map/dot_general | solution.py:459
  (1 shorter events, 0.0 us)
Async XLA Ops:
  0.6 43.6 %copy-start = (bf16[100,1024]{1,0:T(8,128)(2,1)S(1)}, bf16[100,1024]{1,0:T(8,128)(2,1)}, u32[]{:S(2)}) copy-start(bf16[100,1024]{1,0:T(8,128)(2,1)} %readout_hbm.1) | copy-start | bytes 614404
